TPU v7x, 32 devices: a whole 2x2x4 slice. The times are simulated.
32 devices in a mesh: pts: 8 (over z, x), cen: 4 (over y, core).
Axes of the slice: x: 2, y: 2, z: 4, core: 2. Of those that a mesh axis runs over, the one named last changes fastest.
Arguments:
- points: bfloat16 [16384, 768], P('pts'), may hold values from -16 to 16
- centroids: bfloat16 [4096, 768], P('cen'), may hold values from -1 to 1
Outputs:
- new_centroids: bfloat16 [4096, 768], P(('cen', 'pts'))
- distances: float32 [16384], P('pts')
All inputs are finite; a program needn't handle non-finite values.
Results may differ from a plain program's by a relative error of at most 0.0034.
Values may be sent and summed in bfloat16 or wider, within the bound.
A program may use at most 64 MiB of HBM per device.

v0:
```python
import math

import jax
import jax.numpy as jnp
from jax import lax
from jax.sharding import PartitionSpec as P

ITERS = 3


sharpness = 4.0


def merged(value, axis, join):
    pieces = jax.tree.map(lambda part: lax.all_gather(part, axis), value)
    head = jax.tree.map(lambda part: part[0], pieces)
    tail = jax.tree.map(lambda part: part[1:], pieces)
    subtotal, _ = lax.scan(lambda subtotal, piece: (join(subtotal, piece), None), head, tail)
    return subtotal


def logits(points, centroids):
    product = lax.dot_general(
        points, centroids, (((1,), (1,)), ((), ())), preferred_element_type=jnp.float32
    )
    return sharpness * product


def combine_lse(earlier, later):
    joined_max = jnp.maximum(earlier[0], later[0])
    summed = earlier[1] * jnp.exp(earlier[0] - joined_max) + later[1] * jnp.exp(
        later[0] - joined_max
    )
    return (joined_max, summed)


def on_device(points, centroids):
    pts_devices = lax.axis_size("pts")
    total_points = points.shape[0] * pts_devices
    local_centroids = centroids.shape[0]
    total_centroids = local_centroids * lax.axis_size("cen")
    width = points.shape[1]
    stored_scores = logits(points, centroids)

    def current_scores():
        return stored_scores

    col_potential = jnp.zeros((local_centroids,), jnp.float32)
    row_potential = jnp.zeros((points.shape[0],), jnp.float32)
    for iteration in range(ITERS):
        shifted = current_scores() + col_potential[None, :]
        highest = jnp.max(shifted, axis=1)
        summed = jnp.sum(jnp.exp(shifted - highest[:, None]), axis=1)
        highest, summed = merged((highest, summed), "cen", combine_lse)
        row_potential = -math.log(total_points) - (highest + jnp.log(summed))
        shifted = current_scores() + row_potential[:, None]
        highest = lax.pmax(jnp.max(shifted, axis=0), "pts")
        summed = lax.psum(jnp.sum(jnp.exp(shifted - highest[None, :]), axis=0), "pts")
        col_potential = -math.log(total_centroids) - (highest + jnp.log(summed))
    transport = jnp.exp(current_scores() + row_potential[:, None] + col_potential[None, :])
    weights = transport.astype(jnp.bfloat16)
    rows_each = local_centroids // pts_devices
    product = lax.dot_general(
        weights, points, (((0,), (0,)), ((), ())), preferred_element_type=jnp.float32
    )
    partial_sums = total_centroids * product
    gathered_block = lax.psum(partial_sums, "pts").astype(jnp.bfloat16)
    own_rows = lax.dynamic_slice_in_dim(
        gathered_block, lax.axis_index("pts") * rows_each, rows_each, 0
    )
    block_float = gathered_block.astype(jnp.float32)
    squares = jnp.sum(block_float * block_float, axis=1)
    cross_terms = lax.dot_general(
        points, gathered_block, (((1,), (1,)), ((), ())), preferred_element_type=jnp.float32
    )
    numerator = jnp.sum(transport * (squares[None, :] - 2.0 * cross_terms), axis=1)
    row_mass = jnp.sum(transport, axis=1)
    numerator, row_mass = lax.psum((numerator, row_mass), "cen")
    distances = numerator / row_mass / width
    return (own_rows, distances)


def solution(mesh):
    in_specs = (P("pts", None), P("cen", None))
    out_specs = (P(("cen", "pts"), None), P("pts"))
    return jax.shard_map(
        on_device, mesh=mesh, in_specs=in_specs, out_specs=out_specs, check_vma=False
    )
```

profile of v0, /device:TPU:25, one launch (start us, length us, event | category | flops | bytes accessed | tf_op | source)
XLA Modules:
  0.0 349.5 jit_solution(9330836802952767740)
XLA Ops:
  0.6 0.0 copy-start
  0.6 1.9 copy-done
  2.5 7.0 %fusion.10 = (f32[2048]{0:T(1024)S(1)}, f32[2048,1024]{0,1:T(8,128)}) fusion(bf16[2048,768]{1,0:T(8,128)(2,1)S(1)} %copy-done, bf16[1024,768]{1,0:T(8,128)(2,1)} %param.9), kind=kOutput, calls=%fused_computation.39 | convolution fusion | flops 3225417728 | bytes 13115392 | tf_op jit(solution)/shard_map/dot_general | solution.py:23
  9.6 5.7 %all-gather = f32[8192]{0:T(1024)S(1)} all-gather(f32[2048]{0:T(1024)S(1)} %get-tuple-element.136), channel_id=2, replica_groups=mesh['pts'=8,'cen'=4] {'cen'}, dimensions={0}, use_global_device_ids=true | all-gather | bytes 40960 | tf_op jit(solution)/shard_map/all_gather | solution.py:15
  15.2 4.5 %exponential_reduce_fusion.5 = f32[2048]{0:T(1024)S(1)} fusion(f32[2048,1024]{0,1:T(8,128)} %get-tuple-element.137, f32[2048]{0:T(1024)S(1)} %get-tuple-element.136), kind=kLoop, calls=%fused_computation.17 | loop fusion | flops 4192256 | bytes 8404992 | tf_op jit(solution)/shard_map/reduce_sum | solution.py:53
  19.8 5.2 %all-gather.1 = f32[8192]{0:T(1024)S(1)} all-gather(f32[2048]{0:T(1024)S(1)} %exponential_reduce_fusion.5), channel_id=3, replica_groups=mesh['pts'=8,'cen'=4] {'cen'}, dimensions={0}, use_global_device_ids=true | all-gather | bytes 40960 | tf_op jit(solution)/shard_map/all_gather | solution.py:15
  25.0 0.2 while.36
  25.2 4.0 %add_reduce_fusion.3 = f32[1024]{0:T(1024)S(1)} fusion(f32[2048,1024]{0,1:T(8,128)} %get-tuple-element.137, f32[2048]{0:T(1024)S(1)} %add_subtract_fusion.2), kind=kLoop, calls=%fused_computation.21 | loop fusion | flops 4193280 | bytes 8400896 | tf_op jit(solution)/shard_map/reduce_max | solution.py:57
  29.2 13.1 %pmax.21 = f32[1024]{0:T(1024)S(1)} all-reduce(f32[1024]{0:T(1024)S(1)} %add_reduce_fusion.3), channel_id=1, replica_groups=mesh['pts'=8,'cen'=4] {'pts'}, use_global_device_ids=true, to_apply=%region_5.6 | all-reduce | flops 1024 | bytes 8192 | tf_op jit(solution)/shard_map/pmax | solution.py:57
  42.3 4.4 %exponential_reduce_fusion.4 = f32[1024]{0:T(1024)S(1)} fusion(f32[2048,1024]{0,1:T(8,128)} %get-tuple-element.137, f32[1024]{0:T(1024)S(1)} %pmax.21, f32[2048]{0:T(1024)S(1)} %add_subtract_fusion.2), kind=kLoop, calls=%fused_computation.16 | loop fusion | flops 6290432 | bytes 8404992 | tf_op jit(solution)/shard_map/reduce_sum | solution.py:58
  46.7 15.3 %psum.42 = f32[1024]{0:T(1024)S(1)} all-reduce(f32[1024]{0:T(1024)S(1)} %exponential_reduce_fusion.4), channel_id=1, replica_groups=mesh['pts'=8,'cen'=4] {'pts'}, use_global_device_ids=true, to_apply=%region_7.8 | all-reduce | flops 1024 | bytes 8192 | tf_op jit(solution)/shard_map/psum | solution.py:58
  62.0 4.0 %add_reduce_fusion.2 = f32[2048]{0:T(1024)S(1)} fusion(f32[2048,1024]{0,1:T(8,128)} %get-tuple-element.137, f32[1024]{0:T(1024)S(1)} %add_subtract_fusion.5), kind=kLoop, calls=%fused_computation.20 | loop fusion | flops 4192256 | bytes 8400896 | tf_op jit(solution)/shard_map/reduce_max | solution.py:52
  66.0 12.3 %all-gather.2 = f32[8192]{0:T(1024)S(1)} all-gather(f32[2048]{0:T(1024)S(1)} %add_reduce_fusion.2), channel_id=4, replica_groups=mesh['pts'=8,'cen'=4] {'cen'}, dimensions={0}, use_global_device_ids=true | all-gather | bytes 40960 | tf_op jit(solution)/shard_map/all_gather | solution.py:15
  78.3 4.3 %exponential_reduce_fusion.3 = f32[2048]{0:T(1024)S(1)} fusion(f32[2048,1024]{0,1:T(8,128)} %get-tuple-element.137, f32[2048]{0:T(1024)S(1)} %add_reduce_fusion.2, f32[1024]{0:T(1024)S(1)} %add_subtract_fusion.5), kind=kLoop, calls=%fused_computation.15 | loop fusion | flops 6289408 | bytes 8409088 | tf_op jit(solution)/shard_map/reduce_sum | solution.py:53
  82.6 5.2 %all-gather.3 = f32[8192]{0:T(1024)S(1)} all-gather(f32[2048]{0:T(1024)S(1)} %exponential_reduce_fusion.3), channel_id=5, replica_groups=mesh['pts'=8,'cen'=4] {'cen'}, dimensions={0}, use_global_device_ids=true | all-gather | bytes 40960 | tf_op jit(solution)/shard_map/all_gather | solution.py:15
  87.9 0.2 while.37
  88.1 4.0 %add_reduce_fusion.1 = f32[1024]{0:T(1024)S(1)} fusion(f32[2048,1024]{0,1:T(8,128)} %get-tuple-element.137, f32[2048]{0:T(1024)S(1)} %add_subtract_fusion.1), kind=kLoop, calls=%fused_computation.19 | loop fusion | flops 4193280 | bytes 8400896 | tf_op jit(solution)/shard_map/reduce_max | solution.py:57
  92.1 13.9 %pmax.22 = f32[1024]{0:T(1024)S(1)} all-reduce(f32[1024]{0:T(1024)S(1)} %add_reduce_fusion.1), channel_id=1, replica_groups=mesh['pts'=8,'cen'=4] {'pts'}, use_global_device_ids=true, to_apply=%region_13.14 | all-reduce | flops 1024 | bytes 8192 | tf_op jit(solution)/shard_map/pmax | solution.py:57
  105.9 4.4 %exponential_reduce_fusion.2 = f32[1024]{0:T(1024)S(1)} fusion(f32[2048,1024]{0,1:T(8,128)} %get-tuple-element.137, f32[1024]{0:T(1024)S(1)} %pmax.22, f32[2048]{0:T(1024)S(1)} %add_subtract_fusion.1), kind=kLoop, calls=%fused_computation.14 | loop fusion | flops 6290432 | bytes 8404992 | tf_op jit(solution)/shard_map/reduce_sum | solution.py:58
  110.3 15.3 %psum.43 = f32[1024]{0:T(1024)S(1)} all-reduce(f32[1024]{0:T(1024)S(1)} %exponential_reduce_fusion.2), channel_id=1, replica_groups=mesh['pts'=8,'cen'=4] {'pts'}, use_global_device_ids=true, to_apply=%region_15.16 | all-reduce | flops 1024 | bytes 8192 | tf_op jit(solution)/shard_map/psum | solution.py:58
  125.6 4.0 %add_reduce_fusion = f32[2048]{0:T(1024)S(1)} fusion(f32[2048,1024]{0,1:T(8,128)} %get-tuple-element.137, f32[1024]{0:T(1024)S(1)} %add_subtract_fusion.4), kind=kLoop, calls=%fused_computation.18 | loop fusion | flops 4192256 | bytes 8400896 | tf_op jit(solution)/shard_map/reduce_max | solution.py:52
  129.7 12.3 %all-gather.4 = f32[8192]{0:T(1024)S(1)} all-gather(f32[2048]{0:T(1024)S(1)} %add_reduce_fusion), channel_id=6, replica_groups=mesh['pts'=8,'cen'=4] {'cen'}, dimensions={0}, use_global_device_ids=true | all-gather | bytes 40960 | tf_op jit(solution)/shard_map/all_gather | solution.py:15
  141.9 4.3 %exponential_reduce_fusion.1 = f32[2048]{0:T(1024)S(1)} fusion(f32[2048,1024]{0,1:T(8,128)} %get-tuple-element.137, f32[2048]{0:T(1024)S(1)} %add_reduce_fusion, f32[1024]{0:T(1024)S(1)} %add_subtract_fusion.4), kind=kLoop, calls=%fused_computation.13 | loop fusion | flops 6289408 | bytes 8409088 | tf_op jit(solution)/shard_map/reduce_sum | solution.py:53
  146.2 5.2 %all-gather.5 = f32[8192]{0:T(1024)S(1)} all-gather(f32[2048]{0:T(1024)S(1)} %exponential_reduce_fusion.1), channel_id=7, replica_groups=mesh['pts'=8,'cen'=4] {'cen'}, dimensions={0}, use_global_device_ids=true | all-gather | bytes 40960 | tf_op jit(solution)/shard_map/all_gather | solution.py:15
  151.5 0.2 while.38
  151.7 4.0 %add_reduce_fusion.4 = f32[1024]{0:T(1024)S(1)} fusion(f32[2048,1024]{0,1:T(8,128)} %get-tuple-element.137, f32[2048]{0:T(1024)S(1)} %add_subtract_fusion), kind=kLoop, calls=%fused_computation.22 | loop fusion | flops 4193280 | bytes 8400896 | tf_op jit(solution)/shard_map/reduce_max | solution.py:57
  155.7 14.0 %pmax.23 = f32[1024]{0:T(1024)S(1)} all-reduce(f32[1024]{0:T(1024)S(1)} %add_reduce_fusion.4), channel_id=1, replica_groups=mesh['pts'=8,'cen'=4] {'pts'}, use_global_device_ids=true, to_apply=%region_21.22 | all-reduce | flops 1024 | bytes 8192 | tf_op jit(solution)/shard_map/pmax | solution.py:57
  169.7 4.4 %exponential_reduce_fusion = f32[1024]{0:T(1024)S(1)} fusion(f32[2048,1024]{0,1:T(8,128)} %get-tuple-element.137, f32[1024]{0:T(1024)S(1)} %pmax.23, f32[2048]{0:T(1024)S(1)} %add_subtract_fusion), kind=kLoop, calls=%fused_computation.12 | loop fusion | flops 6290432 | bytes 8404992 | tf_op jit(solution)/shard_map/reduce_sum | solution.py:58
  174.1 15.3 %psum.44 = f32[1024]{0:T(1024)S(1)} all-reduce(f32[1024]{0:T(1024)S(1)} %exponential_reduce_fusion), channel_id=1, replica_groups=mesh['pts'=8,'cen'=4] {'pts'}, use_global_device_ids=true, to_apply=%region_23.24 | all-reduce | flops 1024 | bytes 8192 | tf_op jit(solution)/shard_map/psum | solution.py:58
  189.4 8.8 %fusion.7 = f32[1024,768]{1,0:T(8,128)} fusion(bf16[2048,768]{1,0:T(8,128)(2,1)S(1)} %copy-done, f32[2048,1024]{0,1:T(8,128)} %get-tuple-element.137, f32[1024]{0:T(1024)S(1)} %add_subtract_fusion.3, f32[2048]{0:T(1024)S(1)} %add_subtract_fusion), kind=kOutput, calls=%fused_computation.30 | convolution fusion | flops 3228303360 | bytes 14692352 | tf_op jit(solution)/shard_map/dot_general | solution.py:63
  198.2 119.8 %all-reduce.2 = bf16[1024,768]{1,0:T(8,128)(2,1)} all-reduce(f32[1024,768]{1,0:T(8,128)} %fusion.7), channel_id=1, replica_groups=mesh['pts'=8,'cen'=4] {'pts'}, use_global_device_ids=true, to_apply=%region_24.25 | all-reduce | flops 786432 | bytes 4718592 | tf_op jit(solution)/shard_map/psum | solution.py:67
  318.1 0.0 slice-start
  318.1 1.8 constant_dynamic-slice_fusion.6
  319.8 1.8 multiply_reduce_fusion
  321.6 0.0 slice-start.1
  321.6 7.1 %fusion = f32[2048]{0:T(1024)S(1)} fusion(f32[2048,1024]{0,1:T(8,128)} %get-tuple-element.137, bf16[1024,768]{1,0:T(8,128)(2,1)} %all-reduce.2, bf16[2048,768]{1,0:T(8,128)(2,1)S(1)} %copy-done, f32[1024]{0:T(1024)S(1)} %multiply_reduce_fusion, f32[1024]{0:T(1024)S(1)} %add_subtract_fusion.3, f32[2048]{0:T(1024)S(1)} %add_subtract_fusion), kind=kOutput, calls=%fused_computation.10 | convolution fusion | flops 3233806336 | bytes 13131776 | tf_op jit(solution)/shard_map/dot_general | solution.py:73
  328.7 0.0 slice-done
  328.7 0.0 slice-done.1
  328.7 1.8 fusion.1
  330.6 18.3 %all-reduce = (f32[2048]{0:T(1024)S(1)}, f32[2048]{0:T(1024)S(1)}) all-reduce(f32[2048]{0:T(1024)S(1)} %fusion, f32[2048]{0:T(1024)S(1)} %fusion.1), channel_id=1, replica_groups=mesh['pts'=8,'cen'=4] {'cen'}, use_global_device_ids=true, to_apply=%region_27.28 | all-reduce | flops 4096 | bytes 32768 | tf_op jit(solution)/shard_map/psum | solution.py:78
  348.9 0.6 divide_multiply_fusion
  (43 shorter events, 0.5 us)
Async XLA Ops:
  0.6 1.9 copy-start
  318.1 10.6 %slice-start = ((s8[8388608]{0:T(1024)(128)(4,1)}), s8[4194304]{0:T(1024)(128)(4,1)S(1)}, s32[]{:S(2)}) async-start(s8[8388608]{0:T(1024)(128)(4,1)} %bitcast.27), calls=%async_computation | async-start | bytes 8388608
  321.6 7.1 %slice-start.1 = ((s8[8388608]{0:T(1024)(128)(4,1)}), s8[4194304]{0:T(1024)(128)(4,1)S(1)}, s32[]{:S(2)}) async-start(s8[8388608]{0:T(1024)(128)(4,1)} %bitcast.27), calls=%async_computation.1 | async-start | bytes 8388608
where the time goes:
time: 355 us; the launch traced here: 349 us
  blocking collectives  271 us (76%)
  other arithmetic  50.6 us (14%)
  matrix products  22.9 us (6%)
  local copies, waits for them, and re-layouts  3.95 us (1%)
    psum x1, blocking collectives, on_device(): gathered_block = lax.psum(partial_sums, 'pts').astype(jnp.bfloat16)  120 us
    psum x3, blocking collectives, on_device(): lax.psum(jnp.sum(jnp.exp(shifted - highest[None, :]), axis=0), 'pts')  46 us
    all_gather x6, blocking collectives, merged(): pieces = jax.tree.map(lambda part: lax.all_gather(part, axis), value)  45.8 us
    pmax x3, blocking collectives, on_device(): highest = lax.pmax(jnp.max(shifted, axis=0), 'pts')  41 us
    psum x1, blocking collectives, on_device(): numerator, row_mass = lax.psum((numerator, row_mass), 'cen')  18.3 us
    reduce_sum x3, other arithmetic, on_device(): summed = jnp.sum(jnp.exp(shifted - highest[:, None]), axis=1)  13.1 us
    reduce_sum x3, other arithmetic, on_device(): jnp.sum(jnp.exp(shifted - highest[None, :]), axis=0)  13.1 us
    reduce_max x3, other arithmetic, on_device(): highest = lax.pmax(jnp.max(shifted, axis=0), 'pts')  12 us

commit v1 on v0

v1 whole, which is shorter than its diff:
```python
import functools
import math

import jax
import jax.numpy as jnp
from jax import lax
from jax.experimental import pallas as pl
from jax.experimental.pallas import tpu as pltpu
from jax.sharding import PartitionSpec as P

ITERS = 3
SHARPNESS = 4.0
LOG2E = 1.4426950408889634
LANES = 128
NT = (((1,), (1,)), ((), ()))
NN = (((1,), (0,)), ((), ()))


def log2(value):
    return jnp.log(value) * LOG2E


def merged_lse(parts):
    highest = jnp.max(parts, axis=0)
    return highest + log2(jnp.sum(jnp.exp2(parts - highest[None]), axis=0))


def remote(src, dst, send, recv, axis, index):
    return pltpu.make_async_remote_copy(
        src_ref=src, dst_ref=dst, send_sem=send, recv_sem=recv,
        device_id={axis: index}, device_id_type=pl.DeviceIdType.MESH,
    )


def exchange(slots, send, recv, axis, count):
    me = lax.axis_index(axis)

    def copy_to(step):
        peer = lax.rem(me + step, count)
        return remote(slots.at[me], slots.at[me], send.at[peer], recv.at[me], axis, peer)

    def copy_from(step):
        peer = lax.rem(me + step, count)
        return remote(slots.at[peer], slots.at[peer], send.at[peer], recv.at[peer], axis, peer)

    @pl.loop(1, count)
    def _(step):
        copy_to(step).start()

    @pl.loop(1, count)
    def _(step):
        copy_from(step).wait_recv()

    @pl.loop(1, count)
    def _(step):
        copy_to(step).wait_send()


def kernel(
    n_pts, n_cen, total_points, total_centroids,
    points, centroids, new_block, distances,
    scores, weights, products, row_slots, col_slots, final_slots, row_rep, col_rep, part_max, part_sum,
    mass_acc, num_acc, x_out, x_in, z_out, z_in, gathered,
    row_send, row_recv, col_send, col_recv, final_send, final_recv,
    xs_sem, xr_sem, zs_sem, zr_sem, gxs_sem, gxr_sem, gzs_sem, gzr_sem,
):
    n_i, width = points.shape
    n_k = centroids.shape[0]
    rows = n_k // n_pts
    pair = 2 * rows
    groups = n_pts // 2
    i_chunks = n_i // LANES
    k_chunks = n_k // LANES
    me = lax.axis_index("pts")
    mine = lax.axis_index("cen")
    hi = me // 2
    lo = lax.rem(me, 2)
    other = 1 - lo

    barrier = pltpu.get_barrier_semaphore()

    @pl.loop(1, n_pts)
    def _(step):
        pl.semaphore_signal(
            barrier, inc=1, device_id={"pts": lax.rem(me + step, n_pts)}, device_id_type=pl.DeviceIdType.MESH
        )

    @pl.loop(1, n_cen)
    def _(step):
        pl.semaphore_signal(
            barrier, inc=1, device_id={"cen": lax.rem(mine + step, n_cen)}, device_id_type=pl.DeviceIdType.MESH
        )

    def row_lse(start, slot, shifted):
        highest = [None, None]
        total = [None, None]
        for k in range(k_chunks):
            for half in range(2):
                block = scores[pl.ds(k * LANES, LANES), pl.ds(start + half * LANES, LANES)]
                if shifted:
                    block = block + col_rep[pl.ds(k * LANES, LANES), :]
                block = block.reshape(LANES // 8, 8, LANES)
                top = jnp.max(block, axis=0)
                if highest[half] is None:
                    total[half] = jnp.sum(jnp.exp2(block - top[None]), axis=0)
                else:
                    top = jnp.maximum(highest[half], top)
                    total[half] = total[half] * jnp.exp2(highest[half] - top) + jnp.sum(
                        jnp.exp2(block - top[None]), axis=0
                    )
                highest[half] = top
        for half in range(2):
            top = jnp.max(highest[half], axis=0, keepdims=True)
            summed = jnp.sum(total[half] * jnp.exp2(highest[half] - top), axis=0, keepdims=True)
            slot[pl.ds(start // LANES + half, 1), :] = top + log2(summed)

    for iteration in range(ITERS):
        slots = row_slots.at[iteration]

        @pl.loop(0, i_chunks // 2)
        def _(chunk):
            start = pl.multiple_of(chunk * 2 * LANES, 2 * LANES)
            if iteration == 0:
                product = lax.dot_general(
                    centroids[...], points[pl.ds(start, 2 * LANES), :], NT, preferred_element_type=jnp.float32
                )
                scores[:, pl.ds(start, 2 * LANES)] = product * (SHARPNESS * LOG2E)
            row_lse(start, slots.at[mine], iteration > 0)

        if iteration == 0:
            pl.semaphore_wait(barrier, n_pts + n_cen - 2)
        exchange(slots, row_send.at[iteration], row_recv.at[iteration], "cen", n_cen)
        row_potential = -math.log2(total_points) - merged_lse(slots[...])
        for chunk in range(i_chunks):
            row_rep[:, pl.ds(chunk * LANES, LANES)] = jnp.broadcast_to(
                row_potential[chunk : chunk + 1, :], (8, LANES)
            )

        @pl.loop(0, n_k // 16)
        def _(group):
            start = pl.multiple_of(group * 16, 16)
            parts = [
                scores[pl.ds(start, 16), pl.ds(chunk * LANES, LANES)].reshape(2, 8, LANES)
                + row_rep[:, pl.ds(chunk * LANES, LANES)][None]
                for chunk in range(i_chunks)
            ]
            top = functools.reduce(jnp.maximum, parts)
            total = functools.reduce(jnp.add, [jnp.exp2(part - top) for part in parts])
            part_max[pl.ds(start, 16), :] = top.reshape(16, LANES)
            part_sum[pl.ds(start, 16), :] = total.reshape(16, LANES)

        slots = col_slots.at[iteration]
        for chunk in range(k_chunks):
            tops = part_max[pl.ds(chunk * LANES, LANES), :].T
            sums = part_sum[pl.ds(chunk * LANES, LANES), :].T
            top = jnp.max(tops, axis=0, keepdims=True)
            summed = jnp.sum(sums * jnp.exp2(tops - top), axis=0, keepdims=True)
            slots[me, pl.ds(chunk, 1), :] = top + log2(summed)
        exchange(slots, col_send.at[iteration], col_recv.at[iteration], "pts", n_pts)
        col_potential = -math.log2(total_centroids) - merged_lse(slots[...])
        for chunk in range(k_chunks):
            col_rep[pl.ds(chunk * LANES, LANES), :] = jnp.broadcast_to(
                col_potential[chunk : chunk + 1, :], (LANES, LANES)
            ).T

    mass_acc[...] = jnp.zeros_like(mass_acc)
    num_acc[...] = jnp.zeros_like(num_acc)

    def x_copy(group):
        return remote(x_out.at[group], x_in.at[group], xs_sem.at[group], xr_sem.at[group], "pts", 2 * hi + other)

    def z_copy_to(group):
        return remote(z_out.at[group], z_in.at[hi], zs_sem.at[group], zr_sem.at[hi], "pts", 2 * group + lo)

    def z_copy_from(group):
        return remote(z_out.at[group], z_in.at[group], zs_sem.at[group], zr_sem.at[group], "pts", 2 * group + lo)

    @pl.loop(0, groups)
    def _(step):
        group = lax.rem(hi + step + 1, groups)
        base = pl.multiple_of(group * pair, pair)

        @pl.loop(0, pair // 16)
        def _(sub):
            start = pl.multiple_of(base + sub * 16, 16)
            for chunk in range(i_chunks):
                lanes = pl.ds(chunk * LANES, LANES)
                value = (
                    scores[pl.ds(start, 16), lanes].reshape(2, 8, LANES)
                    + row_rep[:, lanes][None]
                    + col_rep[pl.ds(start, 16), :].reshape(2, 8, LANES)
                )
                value = jnp.exp2(value)
                mass_acc[:, lanes] += value[0] + value[1]
                value = value.reshape(16, LANES)
                scores[pl.ds(start, 16), lanes] = value
                weights[pl.ds(start, 16), lanes] = value.astype(jnp.bfloat16)

        products[group] = lax.dot_general(
            weights[pl.ds(base, pair), :], points[...], NN, preferred_element_type=jnp.float32
        )
        x_out[group] = products[group, pl.ds(pl.multiple_of(other * rows, rows), rows), :].astype(jnp.bfloat16)
        x_copy(group).start()

    own_half = pl.ds(pl.multiple_of(lo * rows, rows), rows)

    @pl.loop(0, groups - 1)
    def _(step):
        group = lax.rem(hi + step + 1, groups)
        x_copy(group).wait_recv()
        z_out[group] = (products[group, own_half, :] + x_in[group].astype(jnp.float32)).astype(jnp.bfloat16)
        z_copy_to(group).start()

    x_copy(hi).wait_recv()
    products[hi, own_half, :] = products[hi, own_half, :] + x_in[hi].astype(jnp.float32)

    @pl.loop(0, groups - 1)
    def _(step):
        group = lax.rem(hi + step + 1, groups)
        z_copy_from(group).wait_recv()
        products[hi, own_half, :] = products[hi, own_half, :] + z_in[group].astype(jnp.float32)

    finished = (products[hi, own_half, :] * float(total_centroids)).astype(jnp.bfloat16)
    new_block[...] = finished
    gathered[me] = finished

    def gx_copy(group, side):
        block = gathered.at[2 * group + side]
        return remote(block, block, gxs_sem.at[group], gxr_sem.at[group], "pts", 2 * hi + other)

    def gz_copy_to(group):
        block = gathered.at[me]
        return remote(block, block, gzs_sem.at[group], gzr_sem.at[hi], "pts", 2 * group + lo)

    def gz_copy_from(group):
        block = gathered.at[2 * group + lo]
        return remote(block, block, gzs_sem.at[group], gzr_sem.at[group], "pts", 2 * group + lo)

    gx_copy(hi, lo).start()

    @pl.loop(0, groups - 1)
    def _(step):
        gz_copy_to(lax.rem(hi + step + 1, groups)).start()

    def pair_terms(group):
        base = pl.multiple_of(group * pair, pair)
        block = gathered[pl.ds(2 * group, 2)].reshape(pair, width)
        wide = block.astype(jnp.float32)
        squares = jnp.sum(wide * wide, axis=1, keepdims=True)

        @pl.loop(0, n_i // 512)
        def _(chunk):
            lanes = pl.ds(pl.multiple_of(chunk * 512, 512), 512)
            cross = lax.dot_general(block, points[lanes, :], NT, preferred_element_type=jnp.float32)
            terms = scores[pl.ds(base, pair), lanes] * (squares - 2.0 * cross)
            num_acc[:, lanes] += jnp.sum(terms.reshape(pair // 8, 8, 512), axis=0)

    @pl.loop(0, groups)
    def _(step):
        following = lax.rem(hi + groups - step - 1, groups)
        group = lax.rem(hi + groups - step, groups)

        @pl.when(step < groups - 1)
        def _():
            gz_copy_from(following).wait_recv()
            gx_copy(following, lo).start()

        gx_copy(group, other).wait_recv()
        pair_terms(group)

    final = final_slots.at[mine]
    for chunk in range(i_chunks):
        lanes = pl.ds(chunk * LANES, LANES)
        final[pl.ds(chunk, 1), :] = jnp.sum(num_acc[:, lanes], axis=0, keepdims=True)
        final[pl.ds(i_chunks + chunk, 1), :] = jnp.sum(mass_acc[:, lanes], axis=0, keepdims=True)
    exchange(final_slots, final_send, final_recv, "cen", n_cen)
    sums = jnp.sum(final_slots[...], axis=0)
    distances[...] = sums[:i_chunks] / sums[i_chunks:] / float(width)

    @pl.loop(0, groups)
    def _(step):
        x_copy(step).wait_send()
        gx_copy(step, lo).wait_send()

    @pl.loop(0, groups - 1)
    def _(step):
        group = lax.rem(hi + step + 1, groups)
        z_copy_to(group).wait_send()
        gz_copy_to(group).wait_send()


def on_device(n_pts, n_cen, points, centroids):
    n_i, width = points.shape
    n_k = centroids.shape[0]
    rows, groups = n_k // n_pts, n_pts // 2
    i_chunks, k_chunks = n_i // LANES, n_k // LANES
    f32, bf16 = jnp.float32, jnp.bfloat16
    vmem, dma = pltpu.VMEM, pltpu.SemaphoreType.DMA
    whole = pl.BlockSpec(memory_space=pltpu.VMEM)
    new_block, distances = pl.pallas_call(
        functools.partial(kernel, n_pts, n_cen, n_i * n_pts, n_k * n_cen),
        out_shape=(
            jax.ShapeDtypeStruct((rows, width), bf16),
            jax.ShapeDtypeStruct((i_chunks, LANES), f32),
        ),
        in_specs=[whole, whole],
        out_specs=(whole, whole),
        scratch_shapes=[
            vmem((n_k, n_i), f32),
            vmem((n_k, n_i), bf16),
            vmem((groups, 2 * rows, width), f32),
            vmem((ITERS, n_cen, i_chunks, LANES), f32),
            vmem((ITERS, n_pts, k_chunks, LANES), f32),
            vmem((n_cen, 2 * i_chunks, LANES), f32),
            vmem((8, n_i), f32),
            vmem((n_k, LANES), f32),
            vmem((n_k, LANES), f32),
            vmem((n_k, LANES), f32),
            vmem((8, n_i), f32),
            vmem((8, n_i), f32),
            vmem((groups, rows, width), bf16),
            vmem((groups, rows, width), bf16),
            vmem((groups, rows, width), bf16),
            vmem((groups, rows, width), bf16),
            vmem((n_pts, rows, width), bf16),
            dma((ITERS, n_cen)), dma((ITERS, n_cen)),
            dma((ITERS, n_pts)), dma((ITERS, n_pts)),
            dma((n_cen,)), dma((n_cen,)),
            *[dma((groups,)) for _ in range(8)],
        ],
        compiler_params=pltpu.CompilerParams(
            collective_id=0, has_side_effects=True, vmem_limit_bytes=52 * 2**20
        ),
        cost_estimate=pl.CostEstimate(
            flops=6 * n_i * n_k * width, bytes_accessed=2 * (n_i + n_k) * width, transcendentals=7 * n_i * n_k
        ),
    )(points, centroids)
    return new_block, distances.reshape(n_i)


def solution(mesh):
    n_pts, n_cen = mesh.shape["pts"], mesh.shape["cen"]
    return jax.shard_map(
        functools.partial(on_device, n_pts, n_cen),
        mesh=mesh,
        in_specs=(P("pts", None), P("cen", None)),
        out_specs=(P(("cen", "pts"), None), P("pts")),
        check_vma=False,
    )
```

time: 355 us -> 107 us (0.30); the launches traced: 349 us -> 107 us
  blocking collectives: 271 us -> 0 us
  Pallas kernels: 0 us -> 104 us
  other arithmetic: 50.6 us -> 0 us
  matrix products: 22.9 us -> 0 us
    psum x5 -> x0, blocking collectives: 184 us -> none  [the longest x1 120 us: on_device(): gathered_block = lax.psum(partial_sums, 'pts').astype(jnp.bfloat16)]
    pallas_call x0 -> x1, Pallas kernels: none -> 104 us  [on_device(): pl.pallas_call(functools.partial(kernel, n_pts, n_cen, n_i * n_pts, n_k *...]
    all_gather x6 -> x0, blocking collectives: 45.8 us -> none  [merged(): pieces = jax.tree.map(lambda part: lax.all_gather(part, axis), value)]
    pmax x3 -> x0, blocking collectives: 41 us -> none  [on_device(): highest = lax.pmax(jnp.max(shifted, axis=0), 'pts')]
    reduce_sum x8 -> x0, other arithmetic: 29.8 us -> none  [the longest x3 13.1 us: on_device(): summed = jnp.sum(jnp.exp(shifted - highest[:, None]), axis=1)]
    dot_general x3 -> x0, matrix products: 22.9 us -> none  [the longest x1 8.78 us: on_device(): lax.dot_general(weights, points, (((0,), (0,)), ((), ())), preferred_elem...]
    reduce_max x5 -> x0, other arithmetic: 20 us -> none  [the longest x3 12 us: on_device(): highest = lax.pmax(jnp.max(shifted, axis=0), 'pts')]
where the time goes in v1:
time: 107 us
  Pallas kernels  104 us (97%)
  local copies, waits for them, and re-layouts  2.68 us (3%)
    pallas_call x1, Pallas kernels, on_device(): pl.pallas_call(functools.partial(kernel, n_pts, n_cen, n_i * n_pts, n_k *...  104 us
    unnamed x4, local copies, waits for them, and re-layouts  2.68 us

profile of v1, /device:TPU:25, one launch (start us, length us, event | category | flops | bytes accessed | tf_op | source)
XLA Modules:
  0.0 106.9 jit_solution(6185272036973668000)
XLA Ops:
  0.6 0.0 copy-start
  0.6 1.4 %copy-done = bf16[1024,768]{1,0:T(8,128)(2,1)S(1)} copy-done((bf16[1024,768]{1,0:T(8,128)(2,1)S(1)}, bf16[1024,768]{1,0:T(8,128)(2,1)}, u32[]{:S(2)}) %copy-start) | copy-done | bytes 1572888
  2.0 103.6 %shard_map.41 = (bf16[128,768]{1,0:T(8,128)(2,1)S(1)}, f32[16,128]{1,0:T(8,128)S(1)}) custom-call(bf16[2048,768]{1,0:T(8,128)(2,1)} %points.1, bf16[1024,768]{1,0:T(8,128)(2,1)S(1)} %copy-done), custom_call_target="tpu_custom_call" | custom-call | flops 9663676416 | bytes 4718592 | tf_op jit(solution)/shard_map/pallas_call | solution.py:300
  105.6 0.7 copy.6
  106.3 0.6 copy.7
Async XLA Ops:
  0.6 1.4 %copy-start = (bf16[1024,768]{1,0:T(8,128)(2,1)S(1)}, bf16[1024,768]{1,0:T(8,128)(2,1)}, u32[]{:S(2)}) copy-start(bf16[1024,768]{1,0:T(8,128)(2,1)} %centroids.1) | copy-start | bytes 4718596

commit v2 on v1

v2 whole, which is shorter than its diff:
```python
import functools
import math

import jax
import jax.numpy as jnp
from jax import lax
from jax.experimental import pallas as pl
from jax.experimental.pallas import tpu as pltpu
from jax.sharding import PartitionSpec as P

ITERS = 3
SHARPNESS = 4.0
LOG2E = 1.4426950408889634
LANES = 128
NT = (((1,), (1,)), ((), ()))
NN = (((1,), (0,)), ((), ()))


def log2(value):
    return jnp.log(value) * LOG2E


def merged_lse(parts):
    highest = jnp.max(parts, axis=0)
    return highest + log2(jnp.sum(jnp.exp2(parts - highest[None]), axis=0))


def remote(src, dst, send, recv, axis, index):
    return pltpu.make_async_remote_copy(
        src_ref=src, dst_ref=dst, send_sem=send, recv_sem=recv,
        device_id={axis: index}, device_id_type=pl.DeviceIdType.MESH,
    )


def each(start, stop, body):
    if stop - start <= 8:
        for step in range(start, stop):
            body(step)
    else:
        pl.loop(start, stop)(body)


def tree(join, values):
    values = list(values)
    while len(values) > 1:
        paired = [join(a, b) for a, b in zip(values[::2], values[1::2])]
        values = paired + values[len(values) & ~1 :]
    return values[0]


def exchange(slots, send, recv, axis, count):
    me = lax.axis_index(axis)

    def copy_to(step):
        peer = lax.rem(me + step, count)
        return remote(slots.at[me], slots.at[me], send.at[peer], recv.at[me], axis, peer)

    def copy_from(step):
        peer = lax.rem(me + step, count)
        return remote(slots.at[peer], slots.at[peer], send.at[peer], recv.at[peer], axis, peer)

    each(1, count, lambda step: copy_to(step).start())
    each(1, count, lambda step: copy_from(step).wait_recv())
    each(1, count, lambda step: copy_to(step).wait_send())


def kernel(
    n_pts, n_cen, total_points, total_centroids,
    points, centroids, new_block, distances,
    scores, weights, products, row_slots, col_slots, final_slots, row_rep, col_rep, part_max, part_sum,
    mass_acc, num_acc, x_out, x_in, z_out, z_in, gathered,
    row_send, row_recv, col_send, col_recv, final_send, final_recv,
    xs_sem, xr_sem, zs_sem, zr_sem, gxs_sem, gxr_sem, gzs_sem, gzr_sem,
):
    n_i, width = points.shape
    n_k = centroids.shape[0]
    rows = n_k // n_pts
    pair = 2 * rows
    parts, piece = gathered.shape[0], gathered.shape[3]
    groups = n_pts // 2
    i_chunks = n_i // LANES
    k_chunks = n_k // LANES
    me = lax.axis_index("pts")
    mine = lax.axis_index("cen")
    hi = me // 2
    lo = lax.rem(me, 2)
    other = 1 - lo

    barrier = pltpu.get_barrier_semaphore()

    @pl.loop(1, n_pts)
    def _(step):
        pl.semaphore_signal(
            barrier, inc=1, device_id={"pts": lax.rem(me + step, n_pts)}, device_id_type=pl.DeviceIdType.MESH
        )

    @pl.loop(1, n_cen)
    def _(step):
        pl.semaphore_signal(
            barrier, inc=1, device_id={"cen": lax.rem(mine + step, n_cen)}, device_id_type=pl.DeviceIdType.MESH
        )

    def row_lse(start, slot, block_of):
        highest = [None, None]
        total = [None, None]
        for k in range(k_chunks):
            for half in range(2):
                block = block_of(k, half)
                parts = [block[8 * n : 8 * n + 8] for n in range(LANES // 8)]
                top = tree(jnp.maximum, parts)
                if highest[half] is not None:
                    top = jnp.maximum(highest[half], top)
                summed = tree(jnp.add, [jnp.exp2(part - top) for part in parts])
                if highest[half] is not None:
                    summed = total[half] * jnp.exp2(highest[half] - top) + summed
                highest[half], total[half] = top, summed
        for half in range(2):
            top = jnp.max(highest[half], axis=0, keepdims=True)
            summed = jnp.sum(total[half] * jnp.exp2(highest[half] - top), axis=0, keepdims=True)
            slot[pl.ds(start // LANES + half, 1), :] = top + log2(summed)

    def first_blocks(start):
        columns = points[pl.ds(start, 2 * LANES), :]
        products_of = {}

        def block_of(k, half):
            if k % 2 == 0 and half == 0:
                product = lax.dot_general(
                    centroids[pl.ds(k * LANES, 2 * LANES), :], columns, NT, preferred_element_type=jnp.float32
                ) * (SHARPNESS * LOG2E)
                scores[pl.ds(k * LANES, 2 * LANES), pl.ds(start, 2 * LANES)] = product
                products_of[k // 2] = product
            lines = slice((k % 2) * LANES, (k % 2 + 1) * LANES)
            return products_of[k // 2][lines, half * LANES : (half + 1) * LANES]

        return block_of

    def shifted_blocks(start):
        def block_of(k, half):
            lines = pl.ds(k * LANES, LANES)
            return scores[lines, pl.ds(start + half * LANES, LANES)] + col_rep[lines, :]

        return block_of

    for iteration in range(ITERS):
        slots = row_slots.at[iteration]

        @pl.loop(0, i_chunks // 2)
        def _(chunk):
            start = pl.multiple_of(chunk * 2 * LANES, 2 * LANES)
            row_lse(start, slots.at[mine], shifted_blocks(start) if iteration else first_blocks(start))

        if iteration == 0:
            pl.semaphore_wait(barrier, n_pts + n_cen - 2)
        exchange(slots, row_send.at[iteration], row_recv.at[iteration], "cen", n_cen)
        row_potential = -math.log2(total_points) - merged_lse(slots[...])
        for chunk in range(i_chunks):
            row_rep[:, pl.ds(chunk * LANES, LANES)] = jnp.broadcast_to(
                row_potential[chunk : chunk + 1, :], (8, LANES)
            )

        @pl.loop(0, n_k // 16, unroll=2)
        def _(group):
            start = pl.multiple_of(group * 16, 16)
            parts = [
                scores[pl.ds(start, 16), pl.ds(chunk * LANES, LANES)].reshape(2, 8, LANES)
                + row_rep[:, pl.ds(chunk * LANES, LANES)][None]
                for chunk in range(i_chunks)
            ]
            top = tree(jnp.maximum, parts)
            total = tree(jnp.add, [jnp.exp2(part - top) for part in parts])
            part_max[pl.ds(start, 16), :] = top.reshape(16, LANES)
            part_sum[pl.ds(start, 16), :] = total.reshape(16, LANES)

        slots = col_slots.at[iteration]
        for chunk in range(k_chunks):
            tops = part_max[pl.ds(chunk * LANES, LANES), :].T
            sums = part_sum[pl.ds(chunk * LANES, LANES), :].T
            top = jnp.max(tops, axis=0, keepdims=True)
            summed = jnp.sum(sums * jnp.exp2(tops - top), axis=0, keepdims=True)
            slots[me, pl.ds(chunk, 1), :] = top + log2(summed)
        exchange(slots, col_send.at[iteration], col_recv.at[iteration], "pts", n_pts)
        col_potential = -math.log2(total_centroids) - merged_lse(slots[...])
        for chunk in range(k_chunks):
            col_rep[pl.ds(chunk * LANES, LANES), :] = jnp.broadcast_to(
                col_potential[chunk : chunk + 1, :], (LANES, LANES)
            ).T

    mass_acc[...] = jnp.zeros_like(mass_acc)
    num_acc[...] = jnp.zeros_like(num_acc)

    def x_copy(part, group):
        return remote(
            x_out.at[part, group], x_in.at[part, group], xs_sem.at[part, group], xr_sem.at[part, group],
            "pts", 2 * hi + other,
        )

    def z_copy_to(part, group):
        return remote(
            z_out.at[part, group], z_in.at[part, hi], zs_sem.at[part, group], zr_sem.at[part, hi],
            "pts", 2 * group + lo,
        )

    def z_copy_from(part, group):
        return remote(
            z_out.at[part, group], z_in.at[part, group], zs_sem.at[part, group], zr_sem.at[part, group],
            "pts", 2 * group + lo,
        )

    def gx_copy(part, group, side):
        block = gathered.at[part, 2 * group + side]
        return remote(block, block, gxs_sem.at[part, group], gxr_sem.at[part, group], "pts", 2 * hi + other)

    def gz_copy_to(part, group):
        block = gathered.at[part, me]
        return remote(block, block, gzs_sem.at[part, group], gzr_sem.at[part, hi], "pts", 2 * group + lo)

    def gz_copy_from(part, group):
        block = gathered.at[part, 2 * group + lo]
        return remote(block, block, gzs_sem.at[part, group], gzr_sem.at[part, group], "pts", 2 * group + lo)

    def later(step):
        return lax.rem(hi + step + 1, groups)

    def earlier(step):
        return lax.rem(hi + groups - step - 1, groups)

    own_half = pl.ds(pl.multiple_of(lo * rows, rows), rows)
    other_half = pl.ds(pl.multiple_of(other * rows, rows), rows)

    def columns_of(part):
        return slice(part * piece, (part + 1) * piece)

    def plan(group):
        base = pl.multiple_of(group * pair, pair)

        @pl.loop(0, pair // 16)
        def _(sub):
            start = pl.multiple_of(base + sub * 16, 16)
            for chunk in range(i_chunks):
                lanes = pl.ds(chunk * LANES, LANES)
                value = (
                    scores[pl.ds(start, 16), lanes].reshape(2, 8, LANES)
                    + row_rep[:, lanes][None]
                    + col_rep[pl.ds(start, 16), :].reshape(2, 8, LANES)
                )
                value = jnp.exp2(value)
                mass_acc[:, lanes] += value[0] + value[1]
                value = value.reshape(16, LANES)
                scores[pl.ds(start, 16), lanes] = value
                weights[pl.ds(start, 16), lanes] = value.astype(jnp.bfloat16)

    def produce(part):
        @pl.loop(0, groups)
        def _(step):
            group = later(step)
            if part == 0:
                plan(group)
            base = pl.multiple_of(group * pair, pair)
            products[part, group] = lax.dot_general(
                weights[pl.ds(base, pair), :], points[:, columns_of(part)], NN, preferred_element_type=jnp.float32
            )
            x_out[part, group] = products[part, group, other_half, :].astype(jnp.bfloat16)
            x_copy(part, group).start()

    def reduce_pair(part):
        @pl.loop(0, groups - 1)
        def _(step):
            group = later(step)
            x_copy(part, group).wait_recv()
            z_out[part, group] = (
                products[part, group, own_half, :] + x_in[part, group].astype(jnp.float32)
            ).astype(jnp.bfloat16)
            z_copy_to(part, group).start()

    def finish(part):
        x_copy(part, hi).wait_recv()
        products[part, hi, own_half, :] = products[part, hi, own_half, :] + x_in[part, hi].astype(jnp.float32)

        @pl.loop(0, groups - 1)
        def _(step):
            group = earlier(step)
            z_copy_from(part, group).wait_recv()
            products[part, hi, own_half, :] = products[part, hi, own_half, :] + z_in[part, group].astype(jnp.float32)

        done = (products[part, hi, own_half, :] * float(total_centroids)).astype(jnp.bfloat16)
        new_block[:, columns_of(part)] = done
        gathered[part, me] = done
        gx_copy(part, hi, lo).start()

        @pl.loop(0, groups - 1)
        def _(step):
            gz_copy_to(part, later(step)).start()

    def hand_on(part):
        @pl.loop(0, groups - 1)
        def _(step):
            group = earlier(step)
            gz_copy_from(part, group).wait_recv()
            gx_copy(part, group, lo).start()

    def cross(part):
        @pl.loop(0, groups)
        def _(step):
            group = lax.rem(hi + groups - step, groups)
            gx_copy(part, group, other).wait_recv()
            base = pl.multiple_of(group * pair, pair)
            block = gathered[part, pl.ds(2 * group, 2)].reshape(pair, piece)
            wide = block.astype(jnp.float32)
            squares = jnp.sum(wide * wide, axis=1, keepdims=True)
            doubled = (wide * -2.0).astype(jnp.bfloat16)

            @pl.loop(0, n_i // 512)
            def _(chunk):
                lanes = pl.ds(pl.multiple_of(chunk * 512, 512), 512)
                product = lax.dot_general(
                    doubled, points[lanes, columns_of(part)], NT, preferred_element_type=jnp.float32
                )
                terms = scores[pl.ds(base, pair), lanes] * (squares + product)
                num_acc[:, lanes] += jnp.sum(terms.reshape(pair // 8, 8, 512), axis=0)

    produce(0)
    for part in range(1, parts):
        produce(part)
        reduce_pair(part - 1)
        if part >= 2:
            finish(part - 2)
    reduce_pair(parts - 1)
    if parts >= 2:
        finish(parts - 2)
        hand_on(0)
    finish(parts - 1)
    for part in range(parts):
        if part or parts == 1:
            hand_on(part)
        cross(part)

    final = final_slots.at[mine]
    for chunk in range(i_chunks):
        lanes = pl.ds(chunk * LANES, LANES)
        final[pl.ds(chunk, 1), :] = jnp.sum(num_acc[:, lanes], axis=0, keepdims=True)
        final[pl.ds(i_chunks + chunk, 1), :] = jnp.sum(mass_acc[:, lanes], axis=0, keepdims=True)
    exchange(final_slots, final_send, final_recv, "cen", n_cen)
    sums = jnp.sum(final_slots[...], axis=0)
    distances[...] = sums[:i_chunks] / sums[i_chunks:] / float(width)

    for part in range(parts):

        @pl.loop(0, groups)
        def _(step):
            x_copy(part, step).wait_send()
            gx_copy(part, step, lo).wait_send()

        @pl.loop(0, groups - 1)
        def _(step):
            z_copy_to(part, later(step)).wait_send()
            gz_copy_to(part, later(step)).wait_send()


def on_device(n_pts, n_cen, points, centroids):
    n_i, width = points.shape
    n_k = centroids.shape[0]
    rows, groups = n_k // n_pts, n_pts // 2
    i_chunks, k_chunks = n_i // LANES, n_k // LANES
    parts = 3 if width % (3 * LANES) == 0 else 1
    piece = width // parts
    f32, bf16 = jnp.float32, jnp.bfloat16
    vmem, dma = pltpu.VMEM, pltpu.SemaphoreType.DMA
    whole = pl.BlockSpec(memory_space=pltpu.VMEM)
    new_block, distances = pl.pallas_call(
        functools.partial(kernel, n_pts, n_cen, n_i * n_pts, n_k * n_cen),
        out_shape=(
            jax.ShapeDtypeStruct((rows, width), bf16),
            jax.ShapeDtypeStruct((i_chunks, LANES), f32),
        ),
        in_specs=[whole, whole],
        out_specs=(whole, whole),
        scratch_shapes=[
            vmem((n_k, n_i), f32),
            vmem((n_k, n_i), bf16),
            vmem((parts, groups, 2 * rows, piece), f32),
            vmem((ITERS, n_cen, i_chunks, LANES), f32),
            vmem((ITERS, n_pts, k_chunks, LANES), f32),
            vmem((n_cen, 2 * i_chunks, LANES), f32),
            vmem((8, n_i), f32),
            vmem((n_k, LANES), f32),
            vmem((n_k, LANES), f32),
            vmem((n_k, LANES), f32),
            vmem((8, n_i), f32),
            vmem((8, n_i), f32),
            vmem((parts, groups, rows, piece), bf16),
            vmem((parts, groups, rows, piece), bf16),
            vmem((parts, groups, rows, piece), bf16),
            vmem((parts, groups, rows, piece), bf16),
            vmem((parts, n_pts, rows, piece), bf16),
            dma((ITERS, n_cen)), dma((ITERS, n_cen)),
            dma((ITERS, n_pts)), dma((ITERS, n_pts)),
            dma((n_cen,)), dma((n_cen,)),
            *[dma((parts, groups)) for _ in range(8)],
        ],
        compiler_params=pltpu.CompilerParams(
            collective_id=0, has_side_effects=True, vmem_limit_bytes=52 * 2**20
        ),
        cost_estimate=pl.CostEstimate(
            flops=6 * n_i * n_k * width, bytes_accessed=2 * (n_i + n_k) * width, transcendentals=7 * n_i * n_k
        ),
    )(points, centroids)
    return new_block, distances.reshape(n_i)


def solution(mesh):
    n_pts, n_cen = mesh.shape["pts"], mesh.shape["cen"]
    return jax.shard_map(
        functools.partial(on_device, n_pts, n_cen),
        mesh=mesh,
        in_specs=(P("pts", None), P("cen", None)),
        out_specs=(P(("cen", "pts"), None), P("pts")),
        check_vma=False,
    )
```

time: 107 us -> 101 us (0.944); the launches traced: 107 us -> 99.7 us
  Pallas kernels: 104 us -> 96.4 us
    pallas_call x1, Pallas kernels: 104 us -> 96.4 us  [on_device(): pl.pallas_call(functools.partial(kernel, n_pts, n_cen, n_i * n_pts, n_k *...]
where the time goes in v2:
time: 101 us; the launch traced here: 99.7 us
  Pallas kernels  96.4 us (95%)
  local copies, waits for them, and re-layouts  2.68 us (3%)
    pallas_call x1, Pallas kernels, on_device(): pl.pallas_call(functools.partial(kernel, n_pts, n_cen, n_i * n_pts, n_k *...  96.4 us
    unnamed x4, local copies, waits for them, and re-layouts  2.68 us

profile of v2, /device:TPU:25, one launch (start us, length us, event | category | flops | bytes accessed | tf_op | source)
XLA Modules:
  0.0 99.7 jit_solution(12522417061871863584)
XLA Ops:
  0.6 0.0 copy-start
  0.6 1.4 %copy-done = bf16[1024,768]{1,0:T(8,128)(2,1)S(1)} copy-done((bf16[1024,768]{1,0:T(8,128)(2,1)S(1)}, bf16[1024,768]{1,0:T(8,128)(2,1)}, u32[]{:S(2)}) %copy-start) | copy-done | bytes 1572888
  2.0 96.4 %shard_map.41 = (bf16[128,768]{1,0:T(8,128)(2,1)S(1)}, f32[16,128]{1,0:T(8,128)S(1)}) custom-call(bf16[2048,768]{1,0:T(8,128)(2,1)} %points.1, bf16[1024,768]{1,0:T(8,128)(2,1)S(1)} %copy-done), custom_call_target="tpu_custom_call" | custom-call | flops 9663676416 | bytes 4718592 | tf_op jit(solution)/shard_map/pallas_call | solution.py:370
  98.4 0.7 copy.6
  99.1 0.6 copy.7
Async XLA Ops:
  0.6 1.4 %copy-start = (bf16[1024,768]{1,0:T(8,128)(2,1)S(1)}, bf16[1024,768]{1,0:T(8,128)(2,1)}, u32[]{:S(2)}) copy-start(bf16[1024,768]{1,0:T(8,128)(2,1)} %centroids.1) | copy-start | bytes 4718596

commit v3 on v2

--- a/solution.py
+++ b/solution.py
@@ -65,9 +65,9 @@
 
 
 def kernel(
-    n_pts, n_cen, total_points, total_centroids,
+    scaled, n_pts, n_cen, total_points, total_centroids,
     points, centroids, new_block, distances,
-    scores, weights, products, row_slots, col_slots, final_slots, row_rep, col_rep, part_max, part_sum,
+    scores, weights, products, row_slots, col_slots, final_slots, row_rep, col_rep, part_max, part_sum, row_share,
     mass_acc, num_acc, x_out, x_in, z_out, z_in, gathered,
     row_send, row_recv, col_send, col_recv, final_send, final_recv,
     xs_sem, xr_sem, zs_sem, zr_sem, gxs_sem, gxr_sem, gzs_sem, gzr_sem,
@@ -142,18 +142,69 @@
 
         return block_of
 
+    def first_plan(start, slot):
+        block_of = first_blocks(start)
+        for half in range(2):
+            lanes = pl.ds(start + half * LANES, LANES)
+            top = None
+            for k in range(k_chunks):
+                block = block_of(k, half) if half == 0 else scores[pl.ds(k * LANES, LANES), lanes]
+                here = tree(jnp.maximum, [block[8 * n : 8 * n + 8] for n in range(LANES // 8)])
+                top = here if top is None else jnp.maximum(top, here)
+            top = jnp.max(top, axis=0, keepdims=True)
+            total = None
+            for k in range(k_chunks):
+                value = jnp.exp2(scores[pl.ds(k * LANES, LANES), lanes] - top)
+                scores[pl.ds(k * LANES, LANES), lanes] = value
+                here = tree(jnp.add, [value[8 * n : 8 * n + 8] for n in range(LANES // 8)])
+                total = here if total is None else total + here
+            line = pl.ds(start // LANES + half, 1)
+            row_share[line, :] = top
+            slot[line, :] = top + log2(jnp.sum(total, axis=0, keepdims=True))
+
+    def row_sums(start, slot):
+        for half in range(2):
+            lanes = pl.ds(start + half * LANES, LANES)
+            sums = []
+            for k in range(k_chunks):
+                lines = pl.ds(k * LANES, LANES)
+                value = scores[lines, lanes] * col_rep[lines, :]
+                sums.append(tree(jnp.add, [value[8 * n : 8 * n + 8] for n in range(LANES // 8)]))
+            line = pl.ds(start // LANES + half, 1)
+            slot[line, :] = jnp.sum(tree(jnp.add, sums), axis=0, keepdims=True) * row_share[line, :]
+
+    def poison(sums, least):
+        inside = (sums >= least) & (sums <= 2.0**60)
+        return jnp.sum(jnp.where(inside, 0.0, jnp.nan), keepdims=True)
+
+    row_poison = jnp.zeros((1, 1), jnp.float32)
+    col_poison = jnp.zeros((1, 1), jnp.float32)
     for iteration in range(ITERS):
         slots = row_slots.at[iteration]
 
         @pl.loop(0, i_chunks // 2)
         def _(chunk):
             start = pl.multiple_of(chunk * 2 * LANES, 2 * LANES)
-            row_lse(start, slots.at[mine], shifted_blocks(start) if iteration else first_blocks(start))
+            if not scaled:
+                row_lse(start, slots.at[mine], shifted_blocks(start) if iteration else first_blocks(start))
+            elif iteration == 0:
+                first_plan(start, slots.at[mine])
+            else:
+                row_sums(start, slots.at[mine])
 
         if iteration == 0:
             pl.semaphore_wait(barrier, n_pts + n_cen - 2)
         exchange(slots, row_send.at[iteration], row_recv.at[iteration], "cen", n_cen)
-        row_potential = -math.log2(total_points) - merged_lse(slots[...])
+        if not scaled:
+            row_potential = -math.log2(total_points) - merged_lse(slots[...])
+        elif iteration == 0:
+            share = jnp.exp2(row_share[...] - merged_lse(slots[...]))
+            row_share[...] = share
+            row_potential = share * (1.0 / total_points)
+        else:
+            sums = jnp.sum(slots[...], axis=0)
+            row_poison = row_poison + poison(sums, 2.0**-30)
+            row_potential = row_share[...] / (sums * float(total_points))
         for chunk in range(i_chunks):
             row_rep[:, pl.ds(chunk * LANES, LANES)] = jnp.broadcast_to(
                 row_potential[chunk : chunk + 1, :], (8, LANES)
@@ -162,6 +213,14 @@
         @pl.loop(0, n_k // 16, unroll=2)
         def _(group):
             start = pl.multiple_of(group * 16, 16)
+            if scaled:
+                parts = [
+                    scores[pl.ds(start, 16), pl.ds(chunk * LANES, LANES)].reshape(2, 8, LANES)
+                    * row_rep[:, pl.ds(chunk * LANES, LANES)][None]
+                    for chunk in range(i_chunks)
+                ]
+                part_sum[pl.ds(start, 16), :] = tree(jnp.add, parts).reshape(16, LANES)
+                return
             parts = [
                 scores[pl.ds(start, 16), pl.ds(chunk * LANES, LANES)].reshape(2, 8, LANES)
                 + row_rep[:, pl.ds(chunk * LANES, LANES)][None]
@@ -174,13 +233,22 @@
 
         slots = col_slots.at[iteration]
         for chunk in range(k_chunks):
+            if scaled:
+                sums = jnp.sum(part_sum[pl.ds(chunk * LANES, LANES), :].T, axis=0, keepdims=True)
+                slots[me, pl.ds(chunk, 1), :] = sums + row_poison if iteration == ITERS - 1 else sums
+                continue
             tops = part_max[pl.ds(chunk * LANES, LANES), :].T
             sums = part_sum[pl.ds(chunk * LANES, LANES), :].T
             top = jnp.max(tops, axis=0, keepdims=True)
             summed = jnp.sum(sums * jnp.exp2(tops - top), axis=0, keepdims=True)
             slots[me, pl.ds(chunk, 1), :] = top + log2(summed)
         exchange(slots, col_send.at[iteration], col_recv.at[iteration], "pts", n_pts)
-        col_potential = -math.log2(total_centroids) - merged_lse(slots[...])
+        if scaled:
+            sums = jnp.sum(slots[...], axis=0)
+            col_poison = col_poison + poison(sums, 2.0**-60)
+            col_potential = 1.0 / (sums * float(total_centroids))
+        else:
+            col_potential = -math.log2(total_centroids) - merged_lse(slots[...])
         for chunk in range(k_chunks):
             col_rep[pl.ds(chunk * LANES, LANES), :] = jnp.broadcast_to(
                 col_potential[chunk : chunk + 1, :], (LANES, LANES)
@@ -239,12 +307,9 @@
             start = pl.multiple_of(base + sub * 16, 16)
             for chunk in range(i_chunks):
                 lanes = pl.ds(chunk * LANES, LANES)
-                value = (
-                    scores[pl.ds(start, 16), lanes].reshape(2, 8, LANES)
-                    + row_rep[:, lanes][None]
-                    + col_rep[pl.ds(start, 16), :].reshape(2, 8, LANES)
-                )
-                value = jnp.exp2(value)
+                value = scores[pl.ds(start, 16), lanes].reshape(2, 8, LANES)
+                by_row, by_col = row_rep[:, lanes][None], col_rep[pl.ds(start, 16), :].reshape(2, 8, LANES)
+                value = value * by_row * by_col if scaled else jnp.exp2(value + by_row + by_col)
                 mass_acc[:, lanes] += value[0] + value[1]
                 value = value.reshape(16, LANES)
                 scores[pl.ds(start, 16), lanes] = value
@@ -339,7 +404,9 @@
     for chunk in range(i_chunks):
         lanes = pl.ds(chunk * LANES, LANES)
         final[pl.ds(chunk, 1), :] = jnp.sum(num_acc[:, lanes], axis=0, keepdims=True)
-        final[pl.ds(i_chunks + chunk, 1), :] = jnp.sum(mass_acc[:, lanes], axis=0, keepdims=True)
+        final[pl.ds(i_chunks + chunk, 1), :] = (
+            jnp.sum(mass_acc[:, lanes], axis=0, keepdims=True) + col_poison
+        )
     exchange(final_slots, final_send, final_recv, "cen", n_cen)
     sums = jnp.sum(final_slots[...], axis=0)
     distances[...] = sums[:i_chunks] / sums[i_chunks:] / float(width)
@@ -357,7 +424,7 @@
             gz_copy_to(part, later(step)).wait_send()
 
 
-def on_device(n_pts, n_cen, points, centroids):
+def step_kernel(scaled, n_pts, n_cen, points, centroids):
     n_i, width = points.shape
     n_k = centroids.shape[0]
     rows, groups = n_k // n_pts, n_pts // 2
@@ -368,7 +435,7 @@
     vmem, dma = pltpu.VMEM, pltpu.SemaphoreType.DMA
     whole = pl.BlockSpec(memory_space=pltpu.VMEM)
     new_block, distances = pl.pallas_call(
-        functools.partial(kernel, n_pts, n_cen, n_i * n_pts, n_k * n_cen),
+        functools.partial(kernel, scaled, n_pts, n_cen, n_i * n_pts, n_k * n_cen),
         out_shape=(
             jax.ShapeDtypeStruct((rows, width), bf16),
             jax.ShapeDtypeStruct((i_chunks, LANES), f32),
@@ -386,6 +453,7 @@
             vmem((n_k, LANES), f32),
             vmem((n_k, LANES), f32),
             vmem((n_k, LANES), f32),
+            vmem((i_chunks, LANES), f32),
             vmem((8, n_i), f32),
             vmem((8, n_i), f32),
             vmem((parts, groups, rows, piece), bf16),
@@ -399,13 +467,23 @@
             *[dma((parts, groups)) for _ in range(8)],
         ],
         compiler_params=pltpu.CompilerParams(
-            collective_id=0, has_side_effects=True, vmem_limit_bytes=52 * 2**20
+            collective_id=0 if scaled else 1, has_side_effects=True, vmem_limit_bytes=52 * 2**20
         ),
         cost_estimate=pl.CostEstimate(
             flops=6 * n_i * n_k * width, bytes_accessed=2 * (n_i + n_k) * width, transcendentals=7 * n_i * n_k
         ),
     )(points, centroids)
     return new_block, distances.reshape(n_i)
+
+
+def on_device(n_pts, n_cen, points, centroids):
+    new_block, distances = step_kernel(True, n_pts, n_cen, points, centroids)
+    return lax.cond(
+        distances[0] == distances[0],
+        lambda *_: (new_block, distances),
+        functools.partial(step_kernel, False, n_pts, n_cen),
+        points, centroids,
+    )
 
 
 def solution(mesh):

time: 101 us -> 193 us (1.91)
  Pallas kernels: 96.4 us -> 188 us
    pallas_call x1 -> x2, Pallas kernels: 96.4 us -> 188 us  [step_kernel(): pl.pallas_call(functools.partial(kernel, scaled, n_pts, n_cen, n_i * n_pt...]
where the time goes in v3:
time: 193 us; the launch traced here: 191 us
  Pallas kernels  188 us (97%)
  between operations  1.98 us (1%)
    pallas_call x2, Pallas kernels, step_kernel(): pl.pallas_call(functools.partial(kernel, scaled, n_pts, n_cen, n_i * n_pt...  188 us

profile of v3, /device:TPU:25, one launch (start us, length us, event | category | flops | bytes accessed | tf_op | source)
XLA Modules:
  0.0 191.3 jit_solution(18019630901044242143)
XLA Ops:
  0.6 0.0 copy-start
  0.6 0.0 copy-start.1
  0.6 93.7 %shard_map.43 = (bf16[128,768]{1,0:T(8,128)(2,1)S(1)}, f32[16,128]{1,0:T(8,128)S(1)}) custom-call(bf16[2048,768]{1,0:T(8,128)(2,1)} %points.1, bf16[1024,768]{1,0:T(8,128)(2,1)} %centroids.1), custom_call_target="tpu_custom_call" | custom-call | flops 9663676416 | bytes 4718592 | tf_op jit(solution)/shard_map/pallas_call | solution.py:437
  94.4 0.5 slice.5
  96.2 0.0 copy-done
  96.2 0.0 copy-done.1
  96.2 93.8 %conditional.1 = ((bf16[128,768]{1,0:T(8,128)(2,1)S(1)}, f32[2048]{0:T(1024)S(1)})) conditional(s32[]{:T(128)} %bitcast.2, (bf16[2048,768]{1,0:T(8,128)(2,1)S(1)}, bf16[1024,768]{1,0:T(8,128)(2,1)S(1)}) %tuple.27, (bf16[128,768]{1,0:T(8,128)(2,1)S(1)}, f32[2048]{0:T(1024)S(1)}) %tuple.24), branch_computations={%region_0.0_spmd, %region_1.0_spmd} | conditional | flops 9663676416 | bytes 4718616 | solution.py:481
  96.2 93.8 %branch_0_fun.1 = (bf16[128,768]{1,0:T(8,128)(2,1)S(1)}, f32[16,128]{1,0:T(8,128)S(1)}) custom-call(bf16[2048,768]{1,0:T(8,128)(2,1)S(1)} %get-tuple-element.8.points, bf16[1024,768]{1,0:T(8,128)(2,1)S(1)} %get-tuple-element.9.centroids), custom_call_target="tpu_custom_call" | custom-call | flops 9663676416 | bytes 4718592 | tf_op jit(solution)/shard_map/cond/branch_0_fun/pallas_call | solution.py:437
  190.1 0.7 copy.12
  190.7 0.6 copy.13
Async XLA Ops:
  0.6 95.6 %copy-start = (bf16[2048,768]{1,0:T(8,128)(2,1)S(1)}, bf16[2048,768]{1,0:T(8,128)(2,1)}, u32[]{:S(2)}) copy-start(bf16[2048,768]{1,0:T(8,128)(2,1)} %points.1) | copy-start | bytes 9437188
  0.6 95.6 %copy-start.1 = (bf16[1024,768]{1,0:T(8,128)(2,1)S(1)}, bf16[1024,768]{1,0:T(8,128)(2,1)}, u32[]{:S(2)}) copy-start(bf16[1024,768]{1,0:T(8,128)(2,1)} %centroids.1) | copy-start | bytes 4718596

commit v4 on v3

--- a/solution.py
+++ b/solution.py
@@ -61,7 +61,7 @@
 
     each(1, count, lambda step: copy_to(step).start())
     each(1, count, lambda step: copy_from(step).wait_recv())
-    each(1, count, lambda step: copy_to(step).wait_send())
+    return lambda: each(1, count, lambda step: copy_to(step).wait_send())
 
 
 def kernel(
@@ -177,6 +177,7 @@
         inside = (sums >= least) & (sums <= 2.0**60)
         return jnp.sum(jnp.where(inside, 0.0, jnp.nan), keepdims=True)
 
+    unsent = []
     row_poison = jnp.zeros((1, 1), jnp.float32)
     col_poison = jnp.zeros((1, 1), jnp.float32)
     for iteration in range(ITERS):
@@ -194,7 +195,7 @@
 
         if iteration == 0:
             pl.semaphore_wait(barrier, n_pts + n_cen - 2)
-        exchange(slots, row_send.at[iteration], row_recv.at[iteration], "cen", n_cen)
+        unsent += [exchange(slots, row_send.at[iteration], row_recv.at[iteration], "cen", n_cen)]
         if not scaled:
             row_potential = -math.log2(total_points) - merged_lse(slots[...])
         elif iteration == 0:
@@ -242,7 +243,7 @@
             top = jnp.max(tops, axis=0, keepdims=True)
             summed = jnp.sum(sums * jnp.exp2(tops - top), axis=0, keepdims=True)
             slots[me, pl.ds(chunk, 1), :] = top + log2(summed)
-        exchange(slots, col_send.at[iteration], col_recv.at[iteration], "pts", n_pts)
+        unsent += [exchange(slots, col_send.at[iteration], col_recv.at[iteration], "pts", n_pts)]
         if scaled:
             sums = jnp.sum(slots[...], axis=0)
             col_poison = col_poison + poison(sums, 2.0**-60)
@@ -279,13 +280,31 @@
         block = gathered.at[part, 2 * group + side]
         return remote(block, block, gxs_sem.at[part, group], gxr_sem.at[part, group], "pts", 2 * hi + other)
 
-    def gz_copy_to(part, group):
-        block = gathered.at[part, me]
-        return remote(block, block, gzs_sem.at[part, group], gzr_sem.at[part, hi], "pts", 2 * group + lo)
-
-    def gz_copy_from(part, group):
-        block = gathered.at[part, 2 * group + lo]
-        return remote(block, block, gzs_sem.at[part, group], gzr_sem.at[part, group], "pts", 2 * group + lo)
+    def line_copy(part, side, group, direction):
+        column = lo if side == 0 else other
+        block = gathered.at[part, 2 * group + column]
+        return remote(
+            block, block, gzs_sem.at[4 * part + 2 * side + direction, group], gzr_sem.at[2 * part + side, group],
+            "pts", 2 * (hi + 2 * direction - 1) + lo,
+        )
+
+    def along_line(part, side, group):
+        @pl.when((group <= hi) & (hi + 1 < groups))
+        def _():
+            line_copy(part, side, group, 1).start()
+
+        @pl.when((group >= hi) & (hi >= 1))
+        def _():
+            line_copy(part, side, group, 0).start()
+
+    def nearest(step):
+        near = jnp.minimum(hi, groups - 1 - hi)
+        beside = hi + ((step + 1) // 2) * (2 * lax.rem(step + 1, 2) - 1)
+        rest = jnp.where(hi <= groups - 1 - hi, step, groups - 1 - step)
+        return jnp.where(step <= 2 * near, beside, rest)
+
+    def lo_first(part):
+        return parts > 1 and part == parts - 1
 
     def later(step):
         return lax.rem(hi + step + 1, groups)
@@ -352,37 +371,37 @@
         new_block[:, columns_of(part)] = done
         gathered[part, me] = done
         gx_copy(part, hi, lo).start()
-
-        @pl.loop(0, groups - 1)
-        def _(step):
-            gz_copy_to(part, later(step)).start()
-
-    def hand_on(part):
-        @pl.loop(0, groups - 1)
-        def _(step):
-            group = earlier(step)
-            gz_copy_from(part, group).wait_recv()
+        along_line(part, 0, hi)
+        if lo_first(part):
+            gx_copy(part, hi, other).wait_recv()
+            along_line(part, 1, hi)
+
+    def hand_on(part, step):
+        group = nearest(step)
+        for side in range(2 if lo_first(part) else 1):
+            line_copy(part, side, group, 0).wait_recv()
+            along_line(part, side, group)
+        if not lo_first(part):
             gx_copy(part, group, lo).start()
 
-    def cross(part):
-        @pl.loop(0, groups)
-        def _(step):
-            group = lax.rem(hi + groups - step, groups)
+    def cross(part, step):
+        group = nearest(step)
+        if not lo_first(part):
             gx_copy(part, group, other).wait_recv()
-            base = pl.multiple_of(group * pair, pair)
-            block = gathered[part, pl.ds(2 * group, 2)].reshape(pair, piece)
-            wide = block.astype(jnp.float32)
-            squares = jnp.sum(wide * wide, axis=1, keepdims=True)
-            doubled = (wide * -2.0).astype(jnp.bfloat16)
-
-            @pl.loop(0, n_i // 512)
-            def _(chunk):
-                lanes = pl.ds(pl.multiple_of(chunk * 512, 512), 512)
-                product = lax.dot_general(
-                    doubled, points[lanes, columns_of(part)], NT, preferred_element_type=jnp.float32
-                )
-                terms = scores[pl.ds(base, pair), lanes] * (squares + product)
-                num_acc[:, lanes] += jnp.sum(terms.reshape(pair // 8, 8, 512), axis=0)
+        base = pl.multiple_of(group * pair, pair)
+        block = gathered[part, pl.ds(2 * group, 2)].reshape(pair, piece)
+        wide = block.astype(jnp.float32)
+        squares = jnp.sum(wide * wide, axis=1, keepdims=True)
+        doubled = (wide * -2.0).astype(jnp.bfloat16)
+
+        @pl.loop(0, n_i // 512)
+        def _(chunk):
+            lanes = pl.ds(pl.multiple_of(chunk * 512, 512), 512)
+            product = lax.dot_general(
+                doubled, points[lanes, columns_of(part)], NT, preferred_element_type=jnp.float32
+            )
+            terms = scores[pl.ds(base, pair), lanes] * (squares + product)
+            num_acc[:, lanes] += jnp.sum(terms.reshape(pair // 8, 8, 512), axis=0)
 
     produce(0)
     for part in range(1, parts):
@@ -391,14 +410,34 @@
         if part >= 2:
             finish(part - 2)
     reduce_pair(parts - 1)
-    if parts >= 2:
-        finish(parts - 2)
-        hand_on(0)
-    finish(parts - 1)
-    for part in range(parts):
-        if part or parts == 1:
-            hand_on(part)
-        cross(part)
+    if parts == 3 and groups == 4:
+        hand_on(0, 1)
+        finish(1)
+        hand_on(0, 2)
+        hand_on(1, 1)
+        cross(0, 0)
+        hand_on(0, 3)
+        hand_on(1, 2)
+        cross(0, 1)
+        finish(2)
+        hand_on(1, 3)
+        cross(0, 2)
+        hand_on(2, 1)
+        cross(0, 3)
+        hand_on(2, 2)
+        cross(1, 0)
+        hand_on(2, 3)
+        for step in range(1, 4):
+            cross(1, step)
+        for step in range(4):
+            cross(2, step)
+    else:
+        if parts >= 2:
+            finish(parts - 2)
+        finish(parts - 1)
+        for part in range(parts):
+            pl.loop(1, groups)(functools.partial(hand_on, part))
+            pl.loop(0, groups)(functools.partial(cross, part))
 
     final = final_slots.at[mine]
     for chunk in range(i_chunks):
@@ -407,21 +446,35 @@
         final[pl.ds(i_chunks + chunk, 1), :] = (
             jnp.sum(mass_acc[:, lanes], axis=0, keepdims=True) + col_poison
         )
-    exchange(final_slots, final_send, final_recv, "cen", n_cen)
+    unsent += [exchange(final_slots, final_send, final_recv, "cen", n_cen)]
     sums = jnp.sum(final_slots[...], axis=0)
     distances[...] = sums[:i_chunks] / sums[i_chunks:] / float(width)
 
+    for wait in unsent:
+        wait()
     for part in range(parts):
 
         @pl.loop(0, groups)
         def _(step):
             x_copy(part, step).wait_send()
-            gx_copy(part, step, lo).wait_send()
+            if not lo_first(part):
+                gx_copy(part, step, lo).wait_send()
+            for side in range(2 if lo_first(part) else 1):
+
+                @pl.when((step <= hi) & (hi + 1 < groups))
+                def _():
+                    line_copy(part, side, step, 1).wait_send()
+
+                @pl.when((step >= hi) & (hi >= 1))
+                def _():
+                    line_copy(part, side, step, 0).wait_send()
+
+        if lo_first(part):
+            gx_copy(part, hi, lo).wait_send()
 
         @pl.loop(0, groups - 1)
         def _(step):
             z_copy_to(part, later(step)).wait_send()
-            gz_copy_to(part, later(step)).wait_send()
 
 
 def step_kernel(scaled, n_pts, n_cen, points, centroids):
@@ -464,7 +517,9 @@
             dma((ITERS, n_cen)), dma((ITERS, n_cen)),
             dma((ITERS, n_pts)), dma((ITERS, n_pts)),
             dma((n_cen,)), dma((n_cen,)),
-            *[dma((parts, groups)) for _ in range(8)],
+            *[dma((parts, groups)) for _ in range(6)],
+            dma((4 * parts, groups)),
+            dma((2 * parts, groups)),
         ],
         compiler_params=pltpu.CompilerParams(
             collective_id=0 if scaled else 1, has_side_effects=True, vmem_limit_bytes=52 * 2**20

time: 193 us -> 203 us (1.052)
  Pallas kernels: 188 us -> 196 us
    pallas_call x2, Pallas kernels: 188 us -> 196 us  [step_kernel(): pl.pallas_call(functools.partial(kernel, scaled, n_pts, n_cen, n_i * n_pt...]
where the time goes in v4:
time: 203 us; the launch traced here: 200 us
  Pallas kernels  196 us (97%)
    pallas_call x2, Pallas kernels, step_kernel(): pl.pallas_call(functools.partial(kernel, scaled, n_pts, n_cen, n_i * n_pt...  196 us

profile of v4, /device:TPU:25, one launch (start us, length us, event | category | flops | bytes accessed | tf_op | source)
XLA Modules:
  0.0 200.0 jit_solution(16406764230742673236)
XLA Ops:
  0.6 0.0 copy-start
  0.6 0.0 copy-start.1
  0.6 97.2 %shard_map.43 = (bf16[128,768]{1,0:T(8,128)(2,1)S(1)}, f32[16,128]{1,0:T(8,128)S(1)}) custom-call(bf16[2048,768]{1,0:T(8,128)(2,1)} %points.1, bf16[1024,768]{1,0:T(8,128)(2,1)} %centroids.1), custom_call_target="tpu_custom_call" | custom-call | flops 9663676416 | bytes 4718592 | tf_op jit(solution)/shard_map/pallas_call | solution.py:490
  97.8 0.5 slice.5
  99.7 0.0 copy-done
  99.7 0.0 copy-done.1
  99.7 99.1 %conditional.1 = ((bf16[128,768]{1,0:T(8,128)(2,1)S(1)}, f32[2048]{0:T(1024)S(1)})) conditional(s32[]{:T(128)} %bitcast.2, (bf16[2048,768]{1,0:T(8,128)(2,1)S(1)}, bf16[1024,768]{1,0:T(8,128)(2,1)S(1)}) %tuple.27, (bf16[128,768]{1,0:T(8,128)(2,1)S(1)}, f32[2048]{0:T(1024)S(1)}) %tuple.24), branch_computations={%region_0.0_spmd, %region_1.0_spmd} | conditional | flops 9663676416 | bytes 4718616 | solution.py:536
  99.9 98.9 %branch_0_fun.1 = (bf16[128,768]{1,0:T(8,128)(2,1)S(1)}, f32[16,128]{1,0:T(8,128)S(1)}) custom-call(bf16[2048,768]{1,0:T(8,128)(2,1)S(1)} %get-tuple-element.8.points, bf16[1024,768]{1,0:T(8,128)(2,1)S(1)} %get-tuple-element.9.centroids), custom_call_target="tpu_custom_call" | custom-call | flops 9663676416 | bytes 4718592 | tf_op jit(solution)/shard_map/cond/branch_0_fun/pallas_call | solution.py:490
  198.7 0.7 copy.12
  199.4 0.6 copy.13
Async XLA Ops:
  0.6 99.0 %copy-start = (bf16[2048,768]{1,0:T(8,128)(2,1)S(1)}, bf16[2048,768]{1,0:T(8,128)(2,1)}, u32[]{:S(2)}) copy-start(bf16[2048,768]{1,0:T(8,128)(2,1)} %points.1) | copy-start | bytes 9437188
  0.6 99.0 %copy-start.1 = (bf16[1024,768]{1,0:T(8,128)(2,1)S(1)}, bf16[1024,768]{1,0:T(8,128)(2,1)}, u32[]{:S(2)}) copy-start(bf16[1024,768]{1,0:T(8,128)(2,1)} %centroids.1) | copy-start | bytes 4718596

commit v5 on v3

--- a/solution.py
+++ b/solution.py
@@ -61,7 +61,7 @@
 
     each(1, count, lambda step: copy_to(step).start())
     each(1, count, lambda step: copy_from(step).wait_recv())
-    each(1, count, lambda step: copy_to(step).wait_send())
+    return lambda: each(1, count, lambda step: copy_to(step).wait_send())
 
 
 def kernel(
@@ -177,6 +177,7 @@
         inside = (sums >= least) & (sums <= 2.0**60)
         return jnp.sum(jnp.where(inside, 0.0, jnp.nan), keepdims=True)
 
+    unsent = []
     row_poison = jnp.zeros((1, 1), jnp.float32)
     col_poison = jnp.zeros((1, 1), jnp.float32)
     for iteration in range(ITERS):
@@ -194,7 +195,7 @@
 
         if iteration == 0:
             pl.semaphore_wait(barrier, n_pts + n_cen - 2)
-        exchange(slots, row_send.at[iteration], row_recv.at[iteration], "cen", n_cen)
+        unsent += [exchange(slots, row_send.at[iteration], row_recv.at[iteration], "cen", n_cen)]
         if not scaled:
             row_potential = -math.log2(total_points) - merged_lse(slots[...])
         elif iteration == 0:
@@ -242,7 +243,7 @@
             top = jnp.max(tops, axis=0, keepdims=True)
             summed = jnp.sum(sums * jnp.exp2(tops - top), axis=0, keepdims=True)
             slots[me, pl.ds(chunk, 1), :] = top + log2(summed)
-        exchange(slots, col_send.at[iteration], col_recv.at[iteration], "pts", n_pts)
+        unsent += [exchange(slots, col_send.at[iteration], col_recv.at[iteration], "pts", n_pts)]
         if scaled:
             sums = jnp.sum(slots[...], axis=0)
             col_poison = col_poison + poison(sums, 2.0**-60)
@@ -364,25 +365,23 @@
             gz_copy_from(part, group).wait_recv()
             gx_copy(part, group, lo).start()
 
-    def cross(part):
-        @pl.loop(0, groups)
-        def _(step):
-            group = lax.rem(hi + groups - step, groups)
+    def cross(group):
+        base = pl.multiple_of(group * pair, pair)
+        blocks = []
+        squares = jnp.zeros((pair, 1), jnp.float32)
+        for part in range(parts):
             gx_copy(part, group, other).wait_recv()
-            base = pl.multiple_of(group * pair, pair)
-            block = gathered[part, pl.ds(2 * group, 2)].reshape(pair, piece)
-            wide = block.astype(jnp.float32)
-            squares = jnp.sum(wide * wide, axis=1, keepdims=True)
-            doubled = (wide * -2.0).astype(jnp.bfloat16)
-
-            @pl.loop(0, n_i // 512)
-            def _(chunk):
-                lanes = pl.ds(pl.multiple_of(chunk * 512, 512), 512)
-                product = lax.dot_general(
-                    doubled, points[lanes, columns_of(part)], NT, preferred_element_type=jnp.float32
-                )
-                terms = scores[pl.ds(base, pair), lanes] * (squares + product)
-                num_acc[:, lanes] += jnp.sum(terms.reshape(pair // 8, 8, 512), axis=0)
+            wide = gathered[part, pl.ds(2 * group, 2)].reshape(pair, piece).astype(jnp.float32)
+            squares = squares + jnp.sum(wide * wide, axis=1, keepdims=True)
+            blocks.append((wide * -2.0).astype(jnp.bfloat16))
+        doubled = jnp.concatenate(blocks, axis=1)
+
+        @pl.loop(0, n_i // 512)
+        def _(chunk):
+            lanes = pl.ds(pl.multiple_of(chunk * 512, 512), 512)
+            product = lax.dot_general(doubled, points[lanes, :], NT, preferred_element_type=jnp.float32)
+            terms = scores[pl.ds(base, pair), lanes] * (squares + product)
+            num_acc[:, lanes] += jnp.sum(terms.reshape(pair // 8, 8, 512), axis=0)
 
     produce(0)
     for part in range(1, parts):
@@ -395,10 +394,12 @@
         finish(parts - 2)
         hand_on(0)
     finish(parts - 1)
-    for part in range(parts):
-        if part or parts == 1:
-            hand_on(part)
-        cross(part)
+    for part in range(1 if parts >= 2 else 0, parts):
+        hand_on(part)
+
+    @pl.loop(0, groups)
+    def _(step):
+        cross(lax.rem(hi + groups - step, groups))
 
     final = final_slots.at[mine]
     for chunk in range(i_chunks):
@@ -407,10 +408,12 @@
         final[pl.ds(i_chunks + chunk, 1), :] = (
             jnp.sum(mass_acc[:, lanes], axis=0, keepdims=True) + col_poison
         )
-    exchange(final_slots, final_send, final_recv, "cen", n_cen)
+    unsent += [exchange(final_slots, final_send, final_recv, "cen", n_cen)]
     sums = jnp.sum(final_slots[...], axis=0)
     distances[...] = sums[:i_chunks] / sums[i_chunks:] / float(width)
 
+    for wait in unsent:
+        wait()
     for part in range(parts):
 
         @pl.loop(0, groups)

time: 193 us -> 189 us (0.979)
  Pallas kernels: 188 us -> 185 us
    pallas_call x2, Pallas kernels: 188 us -> 185 us  [step_kernel(): pl.pallas_call(functools.partial(kernel, scaled, n_pts, n_cen, n_i * n_pt...]
where the time goes in v5:
time: 189 us
  Pallas kernels  185 us (98%)
  between operations  1.98 us (1%)
    pallas_call x2, Pallas kernels, step_kernel(): pl.pallas_call(functools.partial(kernel, scaled, n_pts, n_cen, n_i * n_pt...  185 us

profile of v5, /device:TPU:25, one launch (start us, length us, event | category | flops | bytes accessed | tf_op | source)
XLA Modules:
  0.0 188.9 jit_solution(5246004300912658885)
XLA Ops:
  0.6 0.0 copy-start
  0.6 0.0 copy-start.1
  0.6 92.1 %shard_map.43 = (bf16[128,768]{1,0:T(8,128)(2,1)S(1)}, f32[16,128]{1,0:T(8,128)S(1)}) custom-call(bf16[2048,768]{1,0:T(8,128)(2,1)} %points.1, bf16[1024,768]{1,0:T(8,128)(2,1)} %centroids.1), custom_call_target="tpu_custom_call" | custom-call | flops 9663676416 | bytes 4718592 | tf_op jit(solution)/shard_map/pallas_call | solution.py:440
  92.8 0.5 slice.5
  94.6 0.0 copy-done
  94.6 0.0 copy-done.1
  94.6 93.0 %conditional.1 = ((bf16[128,768]{1,0:T(8,128)(2,1)S(1)}, f32[2048]{0:T(1024)S(1)})) conditional(s32[]{:T(128)} %bitcast.2, (bf16[2048,768]{1,0:T(8,128)(2,1)S(1)}, bf16[1024,768]{1,0:T(8,128)(2,1)S(1)}) %tuple.27, (bf16[128,768]{1,0:T(8,128)(2,1)S(1)}, f32[2048]{0:T(1024)S(1)}) %tuple.24), branch_computations={%region_0.0_spmd, %region_1.0_spmd} | conditional | flops 9663676416 | bytes 4718616 | solution.py:484
  94.6 93.0 %branch_0_fun.1 = (bf16[128,768]{1,0:T(8,128)(2,1)S(1)}, f32[16,128]{1,0:T(8,128)S(1)}) custom-call(bf16[2048,768]{1,0:T(8,128)(2,1)S(1)} %get-tuple-element.8.points, bf16[1024,768]{1,0:T(8,128)(2,1)S(1)} %get-tuple-element.9.centroids), custom_call_target="tpu_custom_call" | custom-call | flops 9663676416 | bytes 4718592 | tf_op jit(solution)/shard_map/cond/branch_0_fun/pallas_call | solution.py:440
  187.6 0.7 copy.12
  188.3 0.6 copy.13
Async XLA Ops:
  0.6 94.0 %copy-start = (bf16[2048,768]{1,0:T(8,128)(2,1)S(1)}, bf16[2048,768]{1,0:T(8,128)(2,1)}, u32[]{:S(2)}) copy-start(bf16[2048,768]{1,0:T(8,128)(2,1)} %points.1) | copy-start | bytes 9437188
  0.6 94.0 %copy-start.1 = (bf16[1024,768]{1,0:T(8,128)(2,1)S(1)}, bf16[1024,768]{1,0:T(8,128)(2,1)}, u32[]{:S(2)}) copy-start(bf16[1024,768]{1,0:T(8,128)(2,1)} %centroids.1) | copy-start | bytes 4718596

commit v6 on v5

--- a/solution.py
+++ b/solution.py
@@ -183,15 +183,18 @@
     for iteration in range(ITERS):
         slots = row_slots.at[iteration]
 
-        @pl.loop(0, i_chunks // 2)
-        def _(chunk):
-            start = pl.multiple_of(chunk * 2 * LANES, 2 * LANES)
-            if not scaled:
-                row_lse(start, slots.at[mine], shifted_blocks(start) if iteration else first_blocks(start))
-            elif iteration == 0:
-                first_plan(start, slots.at[mine])
-            else:
-                row_sums(start, slots.at[mine])
+        if scaled and iteration == 0:
+            for chunk in range(i_chunks // 2):
+                first_plan(chunk * 2 * LANES, slots.at[mine])
+        else:
+
+            @pl.loop(0, i_chunks // 2)
+            def _(chunk):
+                start = pl.multiple_of(chunk * 2 * LANES, 2 * LANES)
+                if scaled:
+                    row_sums(start, slots.at[mine])
+                else:
+                    row_lse(start, slots.at[mine], shifted_blocks(start) if iteration else first_blocks(start))
 
         if iteration == 0:
             pl.semaphore_wait(barrier, n_pts + n_cen - 2)

time: 189 us -> 187 us (0.989)
  Pallas kernels: 185 us -> 183 us
    pallas_call x2, Pallas kernels: 185 us -> 183 us  [step_kernel(): pl.pallas_call(functools.partial(kernel, scaled, n_pts, n_cen, n_i * n_pt...]
where the time goes in v6:
time: 187 us
  Pallas kernels  183 us (98%)
  between operations  1.98 us (1%)
    pallas_call x2, Pallas kernels, step_kernel(): pl.pallas_call(functools.partial(kernel, scaled, n_pts, n_cen, n_i * n_pt...  183 us

profile of v6, /device:TPU:25, one launch (start us, length us, event | category | flops | bytes accessed | tf_op | source)
XLA Modules:
  0.0 186.7 jit_solution(1394396308979595396)
XLA Ops:
  0.6 0.0 copy-start
  0.6 0.0 copy-start.1
  0.6 89.7 %shard_map.43 = (bf16[128,768]{1,0:T(8,128)(2,1)S(1)}, f32[16,128]{1,0:T(8,128)S(1)}) custom-call(bf16[2048,768]{1,0:T(8,128)(2,1)} %points.1, bf16[1024,768]{1,0:T(8,128)(2,1)} %centroids.1), custom_call_target="tpu_custom_call" | custom-call | flops 9663676416 | bytes 4718592 | tf_op jit(solution)/shard_map/pallas_call | solution.py:443
  90.4 0.5 slice.5
  92.2 0.0 copy-done
  92.2 0.0 copy-done.1
  92.2 93.2 %conditional.1 = ((bf16[128,768]{1,0:T(8,128)(2,1)S(1)}, f32[2048]{0:T(1024)S(1)})) conditional(s32[]{:T(128)} %bitcast.2, (bf16[2048,768]{1,0:T(8,128)(2,1)S(1)}, bf16[1024,768]{1,0:T(8,128)(2,1)S(1)}) %tuple.27, (bf16[128,768]{1,0:T(8,128)(2,1)S(1)}, f32[2048]{0:T(1024)S(1)}) %tuple.24), branch_computations={%region_0.0_spmd, %region_1.0_spmd} | conditional | flops 9663676416 | bytes 4718616 | solution.py:487
  92.4 93.0 %branch_0_fun.1 = (bf16[128,768]{1,0:T(8,128)(2,1)S(1)}, f32[16,128]{1,0:T(8,128)S(1)}) custom-call(bf16[2048,768]{1,0:T(8,128)(2,1)S(1)} %get-tuple-element.8.points, bf16[1024,768]{1,0:T(8,128)(2,1)S(1)} %get-tuple-element.9.centroids), custom_call_target="tpu_custom_call" | custom-call | flops 9663676416 | bytes 4718592 | tf_op jit(solution)/shard_map/cond/branch_0_fun/pallas_call | solution.py:443
  185.4 0.7 copy.12
  186.1 0.6 copy.13
Async XLA Ops:
  0.6 91.6 %copy-start = (bf16[2048,768]{1,0:T(8,128)(2,1)S(1)}, bf16[2048,768]{1,0:T(8,128)(2,1)}, u32[]{:S(2)}) copy-start(bf16[2048,768]{1,0:T(8,128)(2,1)} %points.1) | copy-start | bytes 9437188
  0.6 91.6 %copy-start.1 = (bf16[1024,768]{1,0:T(8,128)(2,1)S(1)}, bf16[1024,768]{1,0:T(8,128)(2,1)}, u32[]{:S(2)}) copy-start(bf16[1024,768]{1,0:T(8,128)(2,1)} %centroids.1) | copy-start | bytes 4718596
